TPU v7x, 32 devices: a whole 2x2x4 slice. The times are simulated.
32 devices in a mesh: gx: 16 (over z, y, x), gy: 2 (over core).
Axes of the slice: x: 2, y: 2, z: 4, core: 2. Of those that a mesh axis runs over, the one named last changes fastest.
Arguments:
- velocity: float32 [512, 64, 128], P('gx', 'gy'), may hold values from -6 to 6
Outputs:
- coefficients: float32 [512, 64, 128], P('gx', 'gy')
All inputs are finite; a program needn't handle non-finite values.
Results may differ from a plain program's by a relative error of at most 0.00002.
Values sent between devices are 32-bit elements; how exact they have to be, the bound alone decides.
No kernel may reach another device: no remote copies, remote signals or barrier semaphores. Data moves between devices by JAX's collectives and lax.ppermute only.
A program may use at most 128 MiB of HBM per device.

v0:
```python
import functools

import jax
import jax.numpy as jnp
import numpy as np
from jax import lax
from jax.experimental import pallas as pl
from jax.experimental.pallas import tpu as pltpu
from jax.sharding import PartitionSpec as P

LEVELS = 4
STEPS = (-1.586134342, -0.05298011854, 0.8829110762, 0.4435068522)
SCALE = 1.149604398
VMEM_BYTES = 24 * 2**20
FIRST_FLOPS = 10**11
COPIES = 2
BY_MATRIX = 2


def windows(block):
    found = []
    first, last = 0, block - 1
    for _ in range(LEVELS):
        low = first - 4 + (first % 2)
        high = last + 4 - (last % 2)
        found.append((low, high))
        first, last = low // 2, high // 2
    return found


def message(block, rows, to):
    sent, derived = {}, {}
    spans = windows(block)
    base = ends = 0
    for level, (low, high) in enumerate(spans):
        size, height = block >> level, rows >> level
        first, last = (0, block - 1) if level == 0 else (v // 2 for v in spans[level - 1])
        planes = [p for p in range(low, high + 1) if p // size == to]
        if abs(to) == 1:
            sign = to
            edge = last + 2 - last % 2 if to > 0 else first - 2 + first % 2
            far, near = edge + sign, edge - sign
            if far in planes and edge + 2 * sign in planes:
                derived[level, edge + 2 * sign] = (far, None)
            if far in planes and near in planes:
                derived[level, edge] = (far, near)
        at = base
        for plane in planes:
            if (level, plane) not in derived:
                sent[level, plane] = at
                at += height
        ends = max(ends, at)
        if level == 0:
            base = at
    return sent, derived, -(-ends // 8) * 8


def shift_of(level):
    return (0, 0, 1, 3)[level]


def places_of(block):
    found = set()
    for level, (low, high) in enumerate(windows(block)):
        size = block >> level
        found |= set(range(low // size, high // size + 1))
    return sorted(found - {0})


def z_product(value, weights):
    width = value.shape[-1]
    high = value.astype(jnp.bfloat16)
    rest = (value - high.astype(jnp.float32)).astype(jnp.bfloat16)
    both = jnp.concatenate([high, rest], axis=1)
    product = jnp.dot(both, weights, preferred_element_type=jnp.float32)
    return product[:, :width] + product[:, width:]


def lanes_of(width, spacing, parity):
    lane = lax.broadcasted_iota(jnp.int32, (1, width), 1)
    return lax.rem(lane, 2 * spacing) == (spacing if parity else 0)


def z_lift(value, spacing):
    width = value.shape[-1]
    axis = value.ndim - 1
    for step, weight in enumerate(STEPS):
        factor = jnp.where(lanes_of(width, spacing, step % 2 == 0), weight, 0.0)
        around = pltpu.roll(value, spacing, axis) + pltpu.roll(value, width - spacing, axis)
        value = value + factor * around
    return value


def x_lift(planes):
    def plus(one, other):
        return other if one is None else one if other is None else one + other

    planes = dict(planes)
    for step, weight in enumerate(STEPS):
        parity = 1 if step % 2 == 0 else 0
        for index in range(min(planes) - 1, max(planes) + 2):
            if index % 2 == parity:
                around = plus(planes.get(index - 1), planes.get(index + 1))
                if around is not None:
                    planes[index] = plus(planes.get(index), weight * around)
    return planes


def y_lift_split(even, odd):
    count = even.shape[0]
    a, b, c, d = STEPS
    odd = odd + a * (even + pltpu.roll(even, count - 1, 0))
    even = even + b * (pltpu.roll(odd, 1, 0) + odd)
    odd = odd + c * (even + pltpu.roll(even, count - 1, 0))
    even = even + d * (pltpu.roll(odd, 1, 0) + odd)
    return even, odd


def y_lift_whole(value):
    count = value.shape[0]
    row = lax.broadcasted_iota(jnp.int32, (count, 1), 0)
    for step, weight in enumerate(STEPS):
        factor = jnp.where(lax.rem(row, 2) == (1 if step % 2 == 0 else 0), weight, 0.0)
        value = value + factor * (pltpu.roll(value, 1, 0) + pltpu.roll(value, count - 1, 0))
    return value


def scaled_z(value, spacing, at):
    width = value.shape[-1]
    odd, even = lanes_of(width, spacing, True), lanes_of(width, spacing, False)
    return value * jnp.where(odd, at * SCALE, jnp.where(even, at / SCALE, 0.0))


def scaled(value, level, x_odd, y_odd):
    at = (SCALE if x_odd else 1 / SCALE) * (SCALE if y_odd else 1 / SCALE)
    if level < BY_MATRIX:
        return value if x_odd != y_odd else value * at
    return scaled_z(value, 1 << level, at)


def spread_z(source, weights, spread, rows, start, size):
    width = source.shape[-1]
    value = source[start : start + size].reshape(size * rows, width)
    spread[start * rows : (start + size) * rows, :] = z_product(value, weights[...])


def spread_x(block, rows, spread, into, low, base):
    for at in range(0, rows, 8):
        planes = {x: spread[x * rows + at : x * rows + at + 8, :] for x in range(block)}
        for x, value in x_lift(planes).items():
            into[x - low, base + at : base + at + 8, :] = value


def z_weights(width, spacing):
    row = lax.broadcasted_iota(jnp.int32, (width, width), 0)
    lane = lax.broadcasted_iota(jnp.int32, (width, width), 1)
    full = scaled_z(z_lift(jnp.where(row == lane, 1.0, 0.0), spacing), spacing, 1.0)
    high = full.astype(jnp.bfloat16)
    rest = (full - high.astype(jnp.float32)).astype(jnp.bfloat16)
    return high, rest


def own_kernel(block, rows, velocity, into, *refs):
    weights, spread, held, arrived = refs[:BY_MATRIX], *refs[BY_MATRIX:]
    width = held.shape[-1]
    parts = arrived.shape[0]
    size = block // parts
    copies = [
        pltpu.make_async_copy(
            velocity.at[pl.ds(part * size, size)], held.at[pl.ds(part * size, size)], arrived.at[part]
        )
        for part in range(parts)
    ]
    for copy in copies:
        copy.start()
    for level, weight in enumerate(weights):
        high, rest = z_weights(width, 1 << level)
        weight[:width, :width] = high
        weight[:width, width:] = rest
        weight[width:, :width] = high
        weight[width:, width:] = jnp.zeros_like(rest)
    for part, copy in enumerate(copies):
        copy.wait()
        spread_z(held, weights[0], spread, rows, part * size, size)
    spread_x(block, rows, spread, into, windows(block)[0][0], 0)


def message_kernel(block, rows, width, count, places, *refs):
    refs = list(refs)

    def take(number):
        taken = refs[:number]
        del refs[:number]
        return taken

    (_,) = take(1)
    others = take(count - 1)
    weights = take(BY_MATRIX)
    (first,) = take(1)
    own = take(LEVELS)
    messages = dict(zip(places, take(len(places))))
    (spread,) = take(1)
    lifted = [first] + take(LEVELS - 1)
    coarse = take(LEVELS - 1)
    spans = windows(block)
    total = count * rows

    tables = {to: message(block, rows, to) for to in places}
    written = {to: set() for to in places}

    def post(to, at, half, value):
        here = range(at, at + 2 * half, 2)
        if written[to].isdisjoint(here):
            messages[to][pl.ds(at, half, 2), :] = value
        else:
            messages[to][pl.ds(at, half, 2), :] += value
        written[to].update(here)

    def put(level, plane, even, odd):
        half = (rows >> level) // 2
        spacing = 1 << level
        if level < LEVELS - 1 and plane % 2 == 0:
            even = jnp.where(lanes_of(width, spacing, True), even, 0.0)
        to = plane // (block >> level)
        if to == 0:
            own[level][plane, pl.ds(0, half, 2), :] = even
            own[level][plane, pl.ds(1, half, 2), :] = odd
        elif (level, plane) in tables[to][0]:
            at, shift = tables[to][0][level, plane], shift_of(level)
            post(to, at, half, pltpu.roll(even, shift, 1) if shift else even)
            post(to, at + 1, half, pltpu.roll(odd, shift, 1) if shift else odd)

    for level in range(LEVELS):
        low, high = spans[level]
        height = total >> level
        half, mine = height // 2, (rows >> level) // 2
        into = lifted[level]

        if level == 0:
            for part, source in enumerate(others):
                step = min(block, max(1, 512 // rows))
                for x in range(0, block, step):
                    spread_z(source, weights[0], spread, rows, x, step)
                spread_x(block, rows, spread, into, low, (part + 1) * rows)
        else:
            start, stop = spans[level - 1][0] // 2, spans[level - 1][1] // 2 + 1
            source = coarse[level - 1]
            if level < BY_MATRIX:
                size = (stop - start) * height
                for at in range(0, size, 512):
                    end = min(size, at + 512)
                    source[at:end, :] = z_product(source[at:end, :], weights[level][...])
            for at in range(0, height, 8):
                planes = {}
                for x in range(start, stop):
                    row = (x - start) * height + at
                    value = source[row : row + 8, :]
                    planes[x] = value if level < BY_MATRIX else z_lift(value, 1 << level)
                for x, value in x_lift(planes).items():
                    into[x - low, at : at + 8, :] = value

        for plane in range(low, high + 1):
            odd_plane = plane % 2 == 1
            if level == 0 and odd_plane and 0 <= plane < block:
                continue
            at = plane - low
            if half % 8 == 0:
                even, odd = y_lift_split(
                    into[at, pl.ds(0, half, 2), :], into[at, pl.ds(1, half, 2), :]
                )
            else:
                into[at] = y_lift_whole(into[at])
                even, odd = into[at, pl.ds(0, half, 2), :], into[at, pl.ds(1, half, 2), :]
            if level < LEVELS - 1 and not odd_plane:
                even = scaled(even, level, odd_plane, False)
                row = ((plane - low) // 2) * half
                coarse[level][row : row + half, :] = even
                even = even[:mine]
            else:
                even = scaled(even[:mine], level, odd_plane, False)
            put(level, plane, even, scaled(odd[:mine], level, odd_plane, True))

    for to in places:
        for row in range(tables[to][2]):
            if row not in written[to]:
                messages[to][row : row + 1, :] = jnp.zeros((1, width), jnp.float32)


def rest_kernel(block, rows, width, first, kept, *refs):
    coarse, out = refs[:-1], refs[-1]
    low = windows(block)[0][0]
    half, mine = first.shape[1] // 2, rows // 2
    for plane in range(block):
        if plane % 2 == 1:
            even, odd = y_lift_split(
                first[plane - low, pl.ds(0, half, 2), :], first[plane - low, pl.ds(1, half, 2), :]
            )
            out[plane, pl.ds(0, mine, 2), :] = scaled(even[:mine], 0, True, False)
            out[plane, pl.ds(1, mine, 2), :] = scaled(odd[:mine], 0, True, True)
        else:
            out[plane] = kept[plane]
    for level in range(1, LEVELS):
        spacing = 1 << level
        for plane in range(block >> level):
            out[plane * spacing, pl.ds(0, rows >> level, spacing), :] += coarse[level - 1][plane]


def add_kernel(block, rows, places, *refs):
    own, received, out = refs[0], refs[1 : 1 + len(places)], refs[1 + len(places)]
    clean = refs[2 + len(places) :]
    a, b, c, d = STEPS
    width = out.shape[-1]
    out[...] = own[...]

    for to, arrived in zip(places, received):
        sent, derived, length = message(block, rows, to)
        for level in sorted({level for level, _ in sent}):
            spacing, height = 1 << level, rows >> level
            shape = (height, width)
            if level > 0:
                here = [at for (found, _), at in sent.items() if found == level]
                start, stop = min(here), -(-(max(here) + height) // 8) * 8
                value = arrived[start:stop, :]
                if shift_of(level):
                    value = pltpu.roll(value, width - shift_of(level), 1)
                lane = lax.broadcasted_iota(jnp.int32, (1, width), 1)
                value = jnp.where(lax.rem(lane, spacing) == 0, value, 0.0)
                source = clean[level - 1]
                source[: stop - start, :] = value
            else:
                start, source = 0, arrived

            def read(plane):
                at = sent[level, plane] - start
                return source[at : at + height, :]

            def add(plane, value):
                x = (plane - to * (block >> level)) * spacing
                out[x, pl.ds(0, height, spacing), :] += value

            for found, plane in sent:
                if found == level:
                    add(plane, read(plane))
            for (found, plane), (far, near) in derived.items():
                if found == level:
                    if near is None:
                        value = (d / SCALE**2) * read(far)
                    else:
                        value = ((1 / c + d) / SCALE**2) * read(far) + (d / SCALE**2) * read(near)
                    row = lax.broadcasted_iota(jnp.int32, shape, 0)
                    keep = (lax.rem(row, 2) == 1) | lanes_of(width, spacing, True)
                    add(plane, jnp.where(keep, value, 0.0))


def call(body, name, outs, ins, scratch=(), aliases=None, flops=0, spaces=None):
    vmem = pl.BlockSpec(memory_space=pltpu.VMEM)
    f32 = jnp.float32
    shapes = [out if isinstance(out, jax.ShapeDtypeStruct) else jax.ShapeDtypeStruct(out, f32) for out in outs]
    moved = 4 * sum(int(np.prod(shape.shape)) for shape in shapes)
    return pl.pallas_call(
        body,
        out_shape=shapes,
        in_specs=spaces or [vmem] * len(ins),
        out_specs=[vmem] * len(outs),
        scratch_shapes=[pltpu.VMEM(shape, f32) if isinstance(shape, tuple) else shape for shape in scratch],
        input_output_aliases=aliases or {},
        compiler_params=pltpu.CompilerParams(vmem_limit_bytes=VMEM_BYTES),
        cost_estimate=pl.CostEstimate(flops=flops, bytes_accessed=2 * moved, transcendentals=0),
        name=name,
    )(*ins)


def local(velocity):
    block, rows, width = velocity.shape
    around, count = lax.axis_size("gx"), lax.axis_size("gy")
    places = places_of(block)
    spans = windows(block)
    total = count * rows

    others = [
        lax.ppermute(velocity, "gy", [(i, (i - k) % count) for i in range(count)])
        for k in range(1, count)
    ]
    lifted = [
        (high - low + 1, total >> level, width) for level, (low, high) in enumerate(spans)
    ]
    coarse = [
        ((high // 2 - low // 2 + 1) * (total >> (level + 1)), width)
        for level, (low, high) in enumerate(spans[:-1])
    ]
    spread = (block * rows, width)
    owned = [(block >> level, rows >> level, width) for level in range(LEVELS)]

    square = jax.ShapeDtypeStruct((2 * width, 2 * width), jnp.bfloat16)
    first, *weights = call(
        functools.partial(own_kernel, block, rows),
        "lift_own",
        [lifted[0]] + [square] * BY_MATRIX,
        [velocity],
        [spread, velocity.shape, pltpu.SemaphoreType.DMA((COPIES,))],
        spaces=[pl.BlockSpec(memory_space=pltpu.HBM)],
    )
    first, kept, *more = call(
        functools.partial(message_kernel, block, rows, width, count, places),
        "make_messages",
        [lifted[0]] + owned + [(message(block, rows, to)[2], width) for to in places],
        [first] + others + weights,
        [spread] + lifted[1:] + coarse,
        {0: 0},
    )
    own_coarse, sent = more[: LEVELS - 1], dict(zip(places, more[LEVELS - 1 :]))
    received = {
        to: lax.ppermute(sent[to], "gx", [(i, (i + to) % around) for i in range(around)])
        for to in sorted(places, key=lambda to: (to < 0, abs(to)))
    }
    (result,) = call(
        functools.partial(rest_kernel, block, rows, width),
        "finish_own",
        [owned[0]],
        [first, kept] + own_coarse,
    )
    for side in (1, -1):
        here = [to for to in places if to * side > 0]
        (result,) = call(
            functools.partial(add_kernel, block, rows, here),
            "add_received",
            [owned[0]],
            [result] + [received[to] for to in here],
            [(message(block, rows, side)[2], width)] * (LEVELS - 1),
            flops=FIRST_FLOPS if side > 0 else 0,
        )
    return result


def solution(mesh):
    return jax.shard_map(
        local, mesh=mesh, in_specs=(P("gx", "gy", None),), out_specs=P("gx", "gy", None), check_vma=False
    )
```

profile of v0, /device:TPU:0, one launch (start us, length us, event | category | flops | bytes accessed | tf_op | source)
XLA Modules:
  0.0 16.7 jit_solution(12134728254331143750)
XLA Ops:
  0.0 0.5 %collective-permute-start = (f32[32,32,128]{2,1,0:T(8,128)}, f32[32,32,128]{2,1,0:T(8,128)S(1)}, u32[]{:S(2)}, u32[]{:S(2)}) collective-permute-start(f32[32,32,128]{2,1,0:T(8,128)} %velocity.1), channel_id=1, source_target_pairs={{0,1},{1,0},{2,3},{3,2},{4,5},{5,4},{6,7},{7,6},{8,9},{9,8},{10,11... | collective-permute-start | bytes 1572872 | tf_op jit(solution)/shard_map/ppermute | solution.py:381
  0.5 0.0 copy-start
  0.5 1.0 %copy-done = f32[32,32,128]{2,1,0:T(8,128)S(1)} copy-done((f32[32,32,128]{2,1,0:T(8,128)S(1)}, f32[32,32,128]{2,1,0:T(8,128)}, u32[]{:S(2)}) %copy-start) | copy-done | bytes 524312
  1.5 1.1 %lift_own.1 = (f32[39,64,128]{2,1,0:T(8,128)S(1)}, bf16[256,256]{1,0:T(8,128)(2,1)S(1)}, bf16[256,256]{1,0:T(8,128)(2,1)S(1)}) custom-call(f32[32,32,128]{2,1,0:T(8,128)S(1)} %copy-done), custom_call_target="tpu_custom_call" | custom-call | bytes 3604480 | tf_op jit(solution)/shard_map/lift_own/pallas_call | solution.py:360
  2.6 0.0 collective-permute-done.refs_1_
  2.6 1.6 %make_messages.1 = (f32[39,64,128]{2,1,0:T(8,128)S(1)}, f32[32,32,128]{2,1,0:T(8,128)S(1)}, f32[16,16,128]{2,1,0:T(8,128)S(1)}, f32[8,8,128]{2,1,0:T(8,128)S(1)}...) custom-call(f32[39,64,128]{2,1,0:T(8,128)S(1)} %get-tuple-element.17, ...), custom_call_target="tpu_custom_call", output_to_operand_aliasing={{0}: (0, {})} | custom-call | bytes 4218880 | tf_op jit(solution)/shard_map/make_messages/pallas_call | solution.py:360
  4.3 2.5 %collective-permute-start.1 = (f32[112,128]{1,0:T(8,128)S(1)}, f32[112,128]{1,0:T(8,128)S(1)}, u32[]{:S(2)}, u32[]{:S(2)}) collective-permute-start(f32[112,128]{1,0:T(8,128)S(1)} %get-tuple-element.25), channel_id=1, source_target_pairs={{0,2},{2,4},{4,6},{6,8},{8,10},{10,12},{12,14},{14,16},{16,18},{18... | collective-permute-start | bytes 172040 | tf_op jit(solution)/shard_map/ppermute | solution.py:413
  6.8 1.5 %collective-permute-start.2 = (f32[16,128]{1,0:T(8,128)S(1)}, f32[16,128]{1,0:T(8,128)S(1)}, u32[]{:S(2)}, u32[]{:S(2)}) collective-permute-start(f32[16,128]{1,0:T(8,128)S(1)} %get-tuple-element.26), channel_id=1, source_target_pairs={{0,4},{2,6},{4,8},{6,10},{8,12},{10,14},{12,16},{14,18},{16,20},{1... | collective-permute-start | bytes 24584 | tf_op jit(solution)/shard_map/ppermute | solution.py:413
  8.4 3.2 %collective-permute-start.3 = (f32[8,128]{1,0:T(8,128)S(1)}, f32[8,128]{1,0:T(8,128)S(1)}, u32[]{:S(2)}, u32[]{:S(2)}) collective-permute-start(f32[8,128]{1,0:T(8,128)S(1)} %get-tuple-element.27), channel_id=1, source_target_pairs={{0,28},{2,30},{4,0},{6,2},{8,4},{10,6},{12,8},{14,10},{16,12},{18,... | collective-permute-start | bytes 12296 | tf_op jit(solution)/shard_map/ppermute | solution.py:413
  11.6 1.4 %collective-permute-start.4 = (f32[128,128]{1,0:T(8,128)S(1)}, f32[128,128]{1,0:T(8,128)S(1)}, u32[]{:S(2)}, u32[]{:S(2)}) collective-permute-start(f32[128,128]{1,0:T(8,128)S(1)} %get-tuple-element.28), channel_id=1, source_target_pairs={{0,30},{2,0},{4,2},{6,4},{8,6},{10,8},{12,10},{14,12},{16,14},{18,... | collective-permute-start | bytes 196616 | tf_op jit(solution)/shard_map/ppermute | solution.py:413
  12.9 0.2 %finish_own.1.refs_0_ = f32[32,32,128]{2,1,0:T(8,128)S(1)} custom-call(f32[39,64,128]{2,1,0:T(8,128)S(1)} %get-tuple-element.20.first, f32[32,32,128]{2,1,0:T(8,128)S(1)} %get-tuple-element.21.kept, f32[16,16,128]{2,1,0:T(8,128)S(1)} %get-tuple-element.22.refs_0_, f32[8,8,128]{2,1,0:T(8,128)S(1)} %get-tuple-element.23.refs_1_, ...), custom_call_target="tpu_custom_call" | custom-call | bytes 1048576 | tf_op jit(solution)/shard_map/finish_own/pallas_call | solution.py:360
  13.1 0.3 %collective-permute-done.2.refs_2_ = f32[16,128]{1,0:T(8,128)S(1)} collective-permute-done((f32[16,128]{1,0:T(8,128)S(1)}, f32[16,128]{1,0:T(8,128)S(1)}, u32[]{:S(2)}, u32[]{:S(2)}) %collective-permute-start.2) | collective-permute-done | bytes 8224 | tf_op jit(solution)/shard_map/ppermute | solution.py:413
  13.4 0.3 %collective-permute-done.1.refs_1_ = f32[112,128]{1,0:T(8,128)S(1)} collective-permute-done((f32[112,128]{1,0:T(8,128)S(1)}, f32[112,128]{1,0:T(8,128)S(1)}, u32[]{:S(2)}, u32[]{:S(2)}) %collective-permute-start.1) | collective-permute-done | bytes 57376 | tf_op jit(solution)/shard_map/ppermute | solution.py:413
  13.7 0.1 add_received.2.refs_0_
  13.8 0.0 collective-permute-done.3.refs_1_
  13.8 2.0 %collective-permute-done.4.refs_2_ = f32[128,128]{1,0:T(8,128)S(1)} collective-permute-done((f32[128,128]{1,0:T(8,128)S(1)}, f32[128,128]{1,0:T(8,128)S(1)}, u32[]{:S(2)}, u32[]{:S(2)}) %collective-permute-start.4) | collective-permute-done | bytes 65568 | tf_op jit(solution)/shard_map/ppermute | solution.py:413
  15.8 0.9 %add_received.3 = f32[32,32,128]{2,1,0:T(8,128)} custom-call(f32[32,32,128]{2,1,0:T(8,128)S(1)} %add_received.2.refs_0_, f32[8,128]{1,0:T(8,128)S(1)} %collective-permute-done.3.refs_1_, f32[128,128]{1,0:T(8,128)S(1)} %collective-permute-done.4.refs_2_), custom_call_target="tpu_custom_call" | custom-call | bytes 1048576 | tf_op jit(solution)/shard_map/add_received/pallas_call | solution.py:360
Async XLA Ops:
  0.0 2.6 %collective-permute-start = (f32[32,32,128]{2,1,0:T(8,128)}, f32[32,32,128]{2,1,0:T(8,128)S(1)}, u32[]{:S(2)}, u32[]{:S(2)}) collective-permute-start(f32[32,32,128]{2,1,0:T(8,128)} %velocity.1), channel_id=1, source_target_pairs={{0,1},{1,0},{2,3},{3,2},{4,5},{5,4},{6,7},{7,6},{8,9},{9,8},{10,11... | collective-permute-start | bytes 1572872 | tf_op jit(solution)/shard_map/ppermute | solution.py:381
  0.5 1.0 %copy-start = (f32[32,32,128]{2,1,0:T(8,128)S(1)}, f32[32,32,128]{2,1,0:T(8,128)}, u32[]{:S(2)}) copy-start(f32[32,32,128]{2,1,0:T(8,128)} %velocity.1) | copy-start | bytes 1572868
  4.3 9.4 %collective-permute-start.1 = (f32[112,128]{1,0:T(8,128)S(1)}, f32[112,128]{1,0:T(8,128)S(1)}, u32[]{:S(2)}, u32[]{:S(2)}) collective-permute-start(f32[112,128]{1,0:T(8,128)S(1)} %get-tuple-element.25), channel_id=1, source_target_pairs={{0,2},{2,4},{4,6},{6,8},{8,10},{10,12},{12,14},{14,16},{16,18},{18... | collective-permute-start | bytes 172040 | tf_op jit(solution)/shard_map/ppermute | solution.py:413
  6.8 6.6 %collective-permute-start.2 = (f32[16,128]{1,0:T(8,128)S(1)}, f32[16,128]{1,0:T(8,128)S(1)}, u32[]{:S(2)}, u32[]{:S(2)}) collective-permute-start(f32[16,128]{1,0:T(8,128)S(1)} %get-tuple-element.26), channel_id=1, source_target_pairs={{0,4},{2,6},{4,8},{6,10},{8,12},{10,14},{12,16},{14,18},{16,20},{1... | collective-permute-start | bytes 24584 | tf_op jit(solution)/shard_map/ppermute | solution.py:413
  8.4 5.4 %collective-permute-start.3 = (f32[8,128]{1,0:T(8,128)S(1)}, f32[8,128]{1,0:T(8,128)S(1)}, u32[]{:S(2)}, u32[]{:S(2)}) collective-permute-start(f32[8,128]{1,0:T(8,128)S(1)} %get-tuple-element.27), channel_id=1, source_target_pairs={{0,28},{2,30},{4,0},{6,2},{8,4},{10,6},{12,8},{14,10},{16,12},{18,... | collective-permute-start | bytes 12296 | tf_op jit(solution)/shard_map/ppermute | solution.py:413
  11.6 4.3 %collective-permute-start.4 = (f32[128,128]{1,0:T(8,128)S(1)}, f32[128,128]{1,0:T(8,128)S(1)}, u32[]{:S(2)}, u32[]{:S(2)}) collective-permute-start(f32[128,128]{1,0:T(8,128)S(1)} %get-tuple-element.28), channel_id=1, source_target_pairs={{0,30},{2,0},{4,2},{6,4},{8,6},{10,8},{12,10},{14,12},{16,14},{18,... | collective-permute-start | bytes 196616 | tf_op jit(solution)/shard_map/ppermute | solution.py:413
where the time goes:
time: 16.9 us; the launch traced here: 16.7 us
  starting transfers between devices  9.08 us (54%)
  Pallas kernels  3.92 us (23%)
  waiting for transfers between devices  2.63 us (16%)
  local copies, waits for them, and re-layouts  1.04 us (6%)
    ppermute x4, starting transfers between devices, local(): lax.ppermute(sent[to], 'gx', [(i, (i + to) % around) for i in range(aroun...  8.62 us
    pallas_call x5, Pallas kernels, call(): pl.pallas_call(body, out_shape=shapes, in_specs=spaces or [vmem] * len(in...  3.92 us
    ppermute x4, waiting for transfers between devices, local(): lax.ppermute(sent[to], 'gx', [(i, (i + to) % around) for i in range(aroun...  2.63 us
    unnamed x2, local copies, waits for them, and re-layouts  1.04 us
    ppermute x1, starting transfers between devices, local(): lax.ppermute(velocity, 'gy', [(i, (i - k) % count) for i in range(count)])  0.45 us
  transfers between devices with their start and end apart: 5, of which 3 were waited for; matrix products, arithmetic and copies ran while one was open for 0% of the time, Pallas kernels for 8%

commit v1 on v0

--- a/solution.py
+++ b/solution.py
@@ -13,8 +13,6 @@
 SCALE = 1.149604398
 VMEM_BYTES = 24 * 2**20
 FIRST_FLOPS = 10**11
-COPIES = 2
-BY_MATRIX = 2
 
 
 def windows(block):
@@ -81,6 +79,14 @@
     return lax.rem(lane, 2 * spacing) == (spacing if parity else 0)
 
 
+def own_lanes(width, level, high_only):
+    spacing, shift = 1 << level, shift_of(level)
+    lane = lax.broadcasted_iota(jnp.int32, (1, width), 1)
+    if high_only:
+        return lax.rem(lane, 2 * spacing) == spacing + shift
+    return lax.rem(lane, spacing) == shift
+
+
 def z_lift(value, spacing):
     width = value.shape[-1]
     axis = value.ndim - 1
@@ -125,17 +131,15 @@
     return value
 
 
-def scaled_z(value, spacing, at):
+def scaled_z(value, spacing):
     width = value.shape[-1]
     odd, even = lanes_of(width, spacing, True), lanes_of(width, spacing, False)
-    return value * jnp.where(odd, at * SCALE, jnp.where(even, at / SCALE, 0.0))
-
-
-def scaled(value, level, x_odd, y_odd):
+    return value * jnp.where(odd, SCALE, jnp.where(even, 1 / SCALE, 0.0))
+
+
+def scaled(value, x_odd, y_odd):
     at = (SCALE if x_odd else 1 / SCALE) * (SCALE if y_odd else 1 / SCALE)
-    if level < BY_MATRIX:
-        return value if x_odd != y_odd else value * at
-    return scaled_z(value, 1 << level, at)
+    return value if x_odd != y_odd else value * at
 
 
 def spread_z(source, weights, spread, rows, start, size):
@@ -151,37 +155,30 @@
             into[x - low, base + at : base + at + 8, :] = value
 
 
-def z_weights(width, spacing):
+def matrix_kernel(*weights):
+    width = weights[0].shape[0] // 2
     row = lax.broadcasted_iota(jnp.int32, (width, width), 0)
     lane = lax.broadcasted_iota(jnp.int32, (width, width), 1)
-    full = scaled_z(z_lift(jnp.where(row == lane, 1.0, 0.0), spacing), spacing, 1.0)
-    high = full.astype(jnp.bfloat16)
-    rest = (full - high.astype(jnp.float32)).astype(jnp.bfloat16)
-    return high, rest
-
-
-def own_kernel(block, rows, velocity, into, *refs):
-    weights, spread, held, arrived = refs[:BY_MATRIX], *refs[BY_MATRIX:]
-    width = held.shape[-1]
-    parts = arrived.shape[0]
-    size = block // parts
-    copies = [
-        pltpu.make_async_copy(
-            velocity.at[pl.ds(part * size, size)], held.at[pl.ds(part * size, size)], arrived.at[part]
-        )
-        for part in range(parts)
-    ]
-    for copy in copies:
-        copy.start()
-    for level, weight in enumerate(weights):
-        high, rest = z_weights(width, 1 << level)
+    value = jnp.where(row == lane, 1.0, 0.0)
+    full = [scaled_z(z_lift(value, 1), 1), jnp.zeros((width, width), jnp.float32)]
+    for level in range(1, LEVELS):
+        spacing = 1 << level
+        value = scaled_z(z_lift(value, spacing), spacing)
+        full[1] += pltpu.roll(value, shift_of(level), 1) if shift_of(level) else value
+        value = jnp.where(lanes_of(width, spacing, False), value, 0.0)
+    for weight, matrix in zip(weights, full):
+        high = matrix.astype(jnp.bfloat16)
+        rest = (matrix - high.astype(jnp.float32)).astype(jnp.bfloat16)
         weight[:width, :width] = high
         weight[:width, width:] = rest
         weight[width:, :width] = high
         weight[width:, width:] = jnp.zeros_like(rest)
-    for part, copy in enumerate(copies):
-        copy.wait()
-        spread_z(held, weights[0], spread, rows, part * size, size)
+
+
+def own_kernel(block, rows, velocity, weights, into, spread):
+    step = max(1, min(block, 512 // rows))
+    for x in range(0, block, step):
+        spread_z(velocity, weights, spread, rows, x, step)
     spread_x(block, rows, spread, into, windows(block)[0][0], 0)
 
 
@@ -195,7 +192,7 @@
 
     (_,) = take(1)
     others = take(count - 1)
-    weights = take(BY_MATRIX)
+    weights = take(2)
     (first,) = take(1)
     own = take(LEVELS)
     messages = dict(zip(places, take(len(places))))
@@ -218,17 +215,19 @@
 
     def put(level, plane, even, odd):
         half = (rows >> level) // 2
-        spacing = 1 << level
-        if level < LEVELS - 1 and plane % 2 == 0:
-            even = jnp.where(lanes_of(width, spacing, True), even, 0.0)
+        low = level < LEVELS - 1 and plane % 2 == 0
+        if level > 0 or low:
+            even = jnp.where(own_lanes(width, level, low), even, 0.0)
+        if level > 0:
+            odd = jnp.where(own_lanes(width, level, False), odd, 0.0)
         to = plane // (block >> level)
         if to == 0:
             own[level][plane, pl.ds(0, half, 2), :] = even
             own[level][plane, pl.ds(1, half, 2), :] = odd
         elif (level, plane) in tables[to][0]:
-            at, shift = tables[to][0][level, plane], shift_of(level)
-            post(to, at, half, pltpu.roll(even, shift, 1) if shift else even)
-            post(to, at + 1, half, pltpu.roll(odd, shift, 1) if shift else odd)
+            at = tables[to][0][level, plane]
+            post(to, at, half, even)
+            post(to, at + 1, half, odd)
 
     for level in range(LEVELS):
         low, high = spans[level]
@@ -245,7 +244,7 @@
         else:
             start, stop = spans[level - 1][0] // 2, spans[level - 1][1] // 2 + 1
             source = coarse[level - 1]
-            if level < BY_MATRIX:
+            if level == 1:
                 size = (stop - start) * height
                 for at in range(0, size, 512):
                     end = min(size, at + 512)
@@ -254,8 +253,7 @@
                 planes = {}
                 for x in range(start, stop):
                     row = (x - start) * height + at
-                    value = source[row : row + 8, :]
-                    planes[x] = value if level < BY_MATRIX else z_lift(value, 1 << level)
+                    planes[x] = source[row : row + 8, :]
                 for x, value in x_lift(planes).items():
                     into[x - low, at : at + 8, :] = value
 
@@ -272,13 +270,13 @@
                 into[at] = y_lift_whole(into[at])
                 even, odd = into[at, pl.ds(0, half, 2), :], into[at, pl.ds(1, half, 2), :]
             if level < LEVELS - 1 and not odd_plane:
-                even = scaled(even, level, odd_plane, False)
+                even = scaled(even, odd_plane, False)
                 row = ((plane - low) // 2) * half
                 coarse[level][row : row + half, :] = even
                 even = even[:mine]
             else:
-                even = scaled(even[:mine], level, odd_plane, False)
-            put(level, plane, even, scaled(odd[:mine], level, odd_plane, True))
+                even = scaled(even[:mine], odd_plane, False)
+            put(level, plane, even, scaled(odd[:mine], odd_plane, True))
 
     for to in places:
         for row in range(tables[to][2]):
@@ -286,8 +284,26 @@
                 messages[to][row : row + 1, :] = jnp.zeros((1, width), jnp.float32)
 
 
-def rest_kernel(block, rows, width, first, kept, *refs):
-    coarse, out = refs[:-1], refs[-1]
+def touched(block, rows, places):
+    found = set()
+    for to in places:
+        sent, derived, _ = message(block, rows, to)
+        found |= {(plane - to * (block >> level)) << level for level, plane in [*sent, *derived]}
+    return runs_of(found)
+
+
+def runs_of(found):
+    runs = []
+    for x in sorted(found):
+        if runs and runs[-1][1] == x:
+            runs[-1] = (runs[-1][0], x + 1)
+        else:
+            runs.append((x, x + 1))
+    return runs
+
+
+def rest_kernel(block, rows, width, places, first, kept, *refs):
+    coarse, (out, whole, done) = refs[:-3], refs[-3:]
     low = windows(block)[0][0]
     half, mine = first.shape[1] // 2, rows // 2
     for plane in range(block):
@@ -295,22 +311,41 @@
             even, odd = y_lift_split(
                 first[plane - low, pl.ds(0, half, 2), :], first[plane - low, pl.ds(1, half, 2), :]
             )
-            out[plane, pl.ds(0, mine, 2), :] = scaled(even[:mine], 0, True, False)
-            out[plane, pl.ds(1, mine, 2), :] = scaled(odd[:mine], 0, True, True)
+            out[plane, pl.ds(0, mine, 2), :] = scaled(even[:mine], True, False)
+            out[plane, pl.ds(1, mine, 2), :] = scaled(odd[:mine], True, True)
         else:
             out[plane] = kept[plane]
     for level in range(1, LEVELS):
-        spacing = 1 << level
+        spacing, shift = 1 << level, shift_of(level)
         for plane in range(block >> level):
-            out[plane * spacing, pl.ds(0, rows >> level, spacing), :] += coarse[level - 1][plane]
-
-
-def add_kernel(block, rows, places, *refs):
-    own, received, out = refs[0], refs[1 : 1 + len(places)], refs[1 + len(places)]
-    clean = refs[2 + len(places) :]
+            value = coarse[level - 1][plane]
+            if shift:
+                value = pltpu.roll(value, width - shift, 1)
+            out[plane * spacing, pl.ds(0, rows >> level, spacing), :] += value
+    busy = {x for start, stop in touched(block, rows, places) for x in range(start, stop)}
+    copies = [
+        pltpu.make_async_copy(out.at[pl.ds(start, stop - start)], whole.at[pl.ds(start, stop - start)], done.at[n])
+        for n, (start, stop) in enumerate(runs_of(set(range(block)) - busy))
+    ]
+    for copy in copies:
+        copy.start()
+    for copy in copies:
+        copy.wait()
+
+
+def add_kernel(block, rows, places, every, *refs):
+    own, received, refs = refs[0], refs[1 : 1 + len(places)], refs[1 + len(places) :]
+    if every is None:
+        out, *clean = refs
+    else:
+        _, whole, out, done, *clean = refs
     a, b, c, d = STEPS
     width = out.shape[-1]
-    out[...] = own[...]
+    if every is None:
+        out[...] = own[...]
+    else:
+        for start, stop in touched(block, rows, every):
+            out[start:stop] = own[start:stop]
 
     for to, arrived in zip(places, received):
         sent, derived, length = message(block, rows, to)
@@ -351,17 +386,27 @@
                     keep = (lax.rem(row, 2) == 1) | lanes_of(width, spacing, True)
                     add(plane, jnp.where(keep, value, 0.0))
 
-
-def call(body, name, outs, ins, scratch=(), aliases=None, flops=0, spaces=None):
-    vmem = pl.BlockSpec(memory_space=pltpu.VMEM)
+    if every is not None:
+        copies = [
+            pltpu.make_async_copy(out.at[pl.ds(start, stop - start)], whole.at[pl.ds(start, stop - start)], done.at[n])
+            for n, (start, stop) in enumerate(touched(block, rows, every))
+        ]
+        for copy in copies:
+            copy.start()
+        for copy in copies:
+            copy.wait()
+
+
+def call(body, name, outs, ins, scratch=(), aliases=None, flops=0, hbm_out=(), hbm_in=()):
+    vmem, hbm = pl.BlockSpec(memory_space=pltpu.VMEM), pl.BlockSpec(memory_space=pltpu.HBM)
     f32 = jnp.float32
     shapes = [out if isinstance(out, jax.ShapeDtypeStruct) else jax.ShapeDtypeStruct(out, f32) for out in outs]
     moved = 4 * sum(int(np.prod(shape.shape)) for shape in shapes)
     return pl.pallas_call(
         body,
         out_shape=shapes,
-        in_specs=spaces or [vmem] * len(ins),
-        out_specs=[vmem] * len(outs),
+        in_specs=[hbm if n in hbm_in else vmem for n in range(len(ins))],
+        out_specs=[hbm if n in hbm_out else vmem for n in range(len(outs))],
         scratch_shapes=[pltpu.VMEM(shape, f32) if isinstance(shape, tuple) else shape for shape in scratch],
         input_output_aliases=aliases or {},
         compiler_params=pltpu.CompilerParams(vmem_limit_bytes=VMEM_BYTES),
@@ -392,19 +437,19 @@
     owned = [(block >> level, rows >> level, width) for level in range(LEVELS)]
 
     square = jax.ShapeDtypeStruct((2 * width, 2 * width), jnp.bfloat16)
-    first, *weights = call(
+    weights = call(matrix_kernel, "make_matrices", [square] * 2, [])
+    (first,) = call(
         functools.partial(own_kernel, block, rows),
         "lift_own",
-        [lifted[0]] + [square] * BY_MATRIX,
-        [velocity],
-        [spread, velocity.shape, pltpu.SemaphoreType.DMA((COPIES,))],
-        spaces=[pl.BlockSpec(memory_space=pltpu.HBM)],
+        [lifted[0]],
+        [velocity, weights[0]],
+        [spread],
     )
     first, kept, *more = call(
         functools.partial(message_kernel, block, rows, width, count, places),
         "make_messages",
         [lifted[0]] + owned + [(message(block, rows, to)[2], width) for to in places],
-        [first] + others + weights,
+        [first] + others + list(weights),
         [spread] + lifted[1:] + coarse,
         {0: 0},
     )
@@ -413,23 +458,36 @@
         to: lax.ppermute(sent[to], "gx", [(i, (i + to) % around) for i in range(around)])
         for to in sorted(places, key=lambda to: (to < 0, abs(to)))
     }
+    result, whole = call(
+        functools.partial(rest_kernel, block, rows, width, places),
+        "finish_own",
+        [owned[0]] * 2,
+        [first, kept] + own_coarse,
+        [pltpu.SemaphoreType.DMA((block,))],
+        hbm_out=(1,),
+    )
+    clean = [(message(block, rows, -1)[2], width)] * (LEVELS - 1)
+    right = [to for to in places if to > 0]
+    left = [to for to in places if to < 0]
     (result,) = call(
-        functools.partial(rest_kernel, block, rows, width),
-        "finish_own",
+        functools.partial(add_kernel, block, rows, right, None),
+        "add_right",
         [owned[0]],
-        [first, kept] + own_coarse,
-    )
-    for side in (1, -1):
-        here = [to for to in places if to * side > 0]
-        (result,) = call(
-            functools.partial(add_kernel, block, rows, here),
-            "add_received",
-            [owned[0]],
-            [result] + [received[to] for to in here],
-            [(message(block, rows, side)[2], width)] * (LEVELS - 1),
-            flops=FIRST_FLOPS if side > 0 else 0,
-        )
-    return result
+        [result] + [received[to] for to in right],
+        clean,
+        flops=FIRST_FLOPS,
+    )
+    (whole,) = call(
+        functools.partial(add_kernel, block, rows, left, places),
+        "add_left",
+        [owned[0]],
+        [result] + [received[to] for to in left] + [whole],
+        [owned[0], pltpu.SemaphoreType.DMA((block,))] + clean,
+        aliases={1 + len(left): 0},
+        hbm_out=(0,),
+        hbm_in=(1 + len(left),),
+    )
+    return whole
 
 
 def solution(mesh):

time: 16.9 us -> 16.9 us (level)
  Pallas kernels: 3.92 us -> 4.95 us
  waiting for transfers between devices: 2.63 us -> 1.62 us
    pallas_call x5 -> x6, Pallas kernels: 3.92 us -> 4.95 us  [call(): pl.pallas_call(body, out_shape=shapes, in_specs=[hbm if n in hbm_in else...]
    ppermute x4, waiting for transfers between devices: 2.63 us -> 1.62 us  [local(): lax.ppermute(sent[to], 'gx', [(i, (i + to) % around) for i in range(aroun...]
  transfers between devices with their start and end apart: 5 -> 5, of which waited for: 3 -> 1; matrix products, arithmetic and copies ran while one was open for 0% -> 0% of each run, Pallas kernels for 8% -> 16%
where the time goes in v1:
time: 16.9 us; the launch traced here: 16.8 us
  starting transfers between devices  9.08 us (54%)
  Pallas kernels  4.95 us (29%)
  waiting for transfers between devices  1.62 us (10%)
  local copies, waits for them, and re-layouts  1.04 us (6%)
    ppermute x4, starting transfers between devices, local(): lax.ppermute(sent[to], 'gx', [(i, (i + to) % around) for i in range(aroun...  8.63 us
    pallas_call x6, Pallas kernels, call(): pl.pallas_call(body, out_shape=shapes, in_specs=[hbm if n in hbm_in else...  4.95 us
    ppermute x4, waiting for transfers between devices, local(): lax.ppermute(sent[to], 'gx', [(i, (i + to) % around) for i in range(aroun...  1.62 us
    unnamed x2, local copies, waits for them, and re-layouts  1.04 us
    ppermute x1, starting transfers between devices, local(): lax.ppermute(velocity, 'gy', [(i, (i - k) % count) for i in range(count)])  0.45 us
  transfers between devices with their start and end apart: 5, of which 1 were waited for; matrix products, arithmetic and copies ran while one was open for 0% of the time, Pallas kernels for 16%

profile of v1, /device:TPU:0, one launch (start us, length us, event | category | flops | bytes accessed | tf_op | source)
XLA Modules:
  0.0 16.8 jit_solution(15259037996917783671)
XLA Ops:
  0.0 0.5 %collective-permute-start = (f32[32,32,128]{2,1,0:T(8,128)}, f32[32,32,128]{2,1,0:T(8,128)S(1)}, u32[]{:S(2)}, u32[]{:S(2)}) collective-permute-start(f32[32,32,128]{2,1,0:T(8,128)} %velocity.1), channel_id=1, source_target_pairs={{0,1},{1,0},{2,3},{3,2},{4,5},{5,4},{6,7},{7,6},{8,9},{9,8},{10,11... | collective-permute-start | bytes 1572872 | tf_op jit(solution)/shard_map/ppermute | solution.py:426
  0.5 1.2 %make_matrices.1 = (bf16[256,256]{1,0:T(8,128)(2,1)S(1)}, bf16[256,256]{1,0:T(8,128)(2,1)S(1)}) custom-call(), custom_call_target="tpu_custom_call" | custom-call | bytes 1048576 | tf_op jit(solution)/shard_map/make_matrices/pallas_call | solution.py:405
  1.6 0.0 copy-start
  1.7 1.0 %copy-done = f32[32,32,128]{2,1,0:T(8,128)S(1)} copy-done((f32[32,32,128]{2,1,0:T(8,128)S(1)}, f32[32,32,128]{2,1,0:T(8,128)}, u32[]{:S(2)}) %copy-start) | copy-done | bytes 524312
  2.7 0.3 %lift_own.1.refs_0_ = f32[39,64,128]{2,1,0:T(8,128)S(1)} custom-call(f32[32,32,128]{2,1,0:T(8,128)S(1)} %copy-done, bf16[256,256]{1,0:T(8,128)(2,1)S(1)} %get-tuple-element.18.weights.refs_2_), custom_call_target="tpu_custom_call" | custom-call | bytes 2555904 | tf_op jit(solution)/shard_map/lift_own/pallas_call | solution.py:405
  3.0 0.0 collective-permute-done.refs_1_
  3.0 1.1 %make_messages.1 = (f32[39,64,128]{2,1,0:T(8,128)S(1)}, f32[32,32,128]{2,1,0:T(8,128)S(1)}, f32[16,16,128]{2,1,0:T(8,128)S(1)}, f32[8,8,128]{2,1,0:T(8,128)S(1)}...) custom-call(f32[39,64,128]{2,1,0:T(8,128)S(1)} %lift_own.1.refs_0_, ...), custom_call_target="tpu_custom_call", output_to_operand_aliasing={{0}: (0, {})} | custom-call | bytes 4218880 | tf_op jit(solution)/shard_map/make_messages/pallas_call | solution.py:405
  4.2 2.5 %collective-permute-start.1 = (f32[112,128]{1,0:T(8,128)S(1)}, f32[112,128]{1,0:T(8,128)S(1)}, u32[]{:S(2)}, u32[]{:S(2)}) collective-permute-start(f32[112,128]{1,0:T(8,128)S(1)} %get-tuple-element.26), channel_id=1, source_target_pairs={{0,2},{2,4},{4,6},{6,8},{8,10},{10,12},{12,14},{14,16},{16,18},{18... | collective-permute-start | bytes 172040 | tf_op jit(solution)/shard_map/ppermute | solution.py:458
  6.7 1.5 %collective-permute-start.2 = (f32[16,128]{1,0:T(8,128)S(1)}, f32[16,128]{1,0:T(8,128)S(1)}, u32[]{:S(2)}, u32[]{:S(2)}) collective-permute-start(f32[16,128]{1,0:T(8,128)S(1)} %get-tuple-element.27), channel_id=1, source_target_pairs={{0,4},{2,6},{4,8},{6,10},{8,12},{10,14},{12,16},{14,18},{16,20},{1... | collective-permute-start | bytes 24584 | tf_op jit(solution)/shard_map/ppermute | solution.py:458
  8.2 3.2 %collective-permute-start.3 = (f32[8,128]{1,0:T(8,128)S(1)}, f32[8,128]{1,0:T(8,128)S(1)}, u32[]{:S(2)}, u32[]{:S(2)}) collective-permute-start(f32[8,128]{1,0:T(8,128)S(1)} %get-tuple-element.28), channel_id=1, source_target_pairs={{0,28},{2,30},{4,0},{6,2},{8,4},{10,6},{12,8},{14,10},{16,12},{18,... | collective-permute-start | bytes 12296 | tf_op jit(solution)/shard_map/ppermute | solution.py:458
  11.4 1.4 %collective-permute-start.4 = (f32[128,128]{1,0:T(8,128)S(1)}, f32[128,128]{1,0:T(8,128)S(1)}, u32[]{:S(2)}, u32[]{:S(2)}) collective-permute-start(f32[128,128]{1,0:T(8,128)S(1)} %get-tuple-element.29), channel_id=1, source_target_pairs={{0,30},{2,0},{4,2},{6,4},{8,6},{10,8},{12,10},{14,12},{16,14},{18,... | collective-permute-start | bytes 196616 | tf_op jit(solution)/shard_map/ppermute | solution.py:458
  12.8 1.2 %finish_own.1 = (f32[32,32,128]{2,1,0:T(8,128)S(1)}, f32[32,32,128]{2,1,0:T(8,128)}) custom-call(f32[39,64,128]{2,1,0:T(8,128)S(1)} %get-tuple-element.20.first, f32[32,32,128]{2,1,0:T(8,128)S(1)} %get-tuple-element.21.kept, f32[16,16,128]{2,1,0:T(8,128)S(1)} %get-tuple-element.22.refs_0_, f32[8,8,128]{2,1,0:T(8,128)S(1)} %get-tuple-element.23.refs_1_, ...), custom_call_target="tpu_custom_call" | custom-call | bytes 2097152 | tf_op jit(solution)/shard_map/finish_own/pallas_call | solution.py:405
  14.0 0.0 collective-permute-done.2.refs_2_
  14.0 0.0 collective-permute-done.1.refs_1_
  14.0 0.1 add_right.1.refs_0_
  14.1 0.0 collective-permute-done.3.refs_1_
  14.1 1.6 %collective-permute-done.4.refs_2_ = f32[128,128]{1,0:T(8,128)S(1)} collective-permute-done((f32[128,128]{1,0:T(8,128)S(1)}, f32[128,128]{1,0:T(8,128)S(1)}, u32[]{:S(2)}, u32[]{:S(2)}) %collective-permute-start.4) | collective-permute-done | bytes 65568 | tf_op jit(solution)/shard_map/ppermute | solution.py:458
  15.7 1.1 %add_left.1 = f32[32,32,128]{2,1,0:T(8,128)} custom-call(f32[32,32,128]{2,1,0:T(8,128)S(1)} %add_right.1.refs_0_, f32[8,128]{1,0:T(8,128)S(1)} %collective-permute-done.3.refs_1_, f32[128,128]{1,0:T(8,128)S(1)} %collective-permute-done.4.refs_2_, f32[32,32,128]{2,1,0:T(8,128)} %get-tuple-element.30.refs_3_), custom_call_target="tpu_custom_call", output_to_operand_aliasing={{}: (3, {})} | custom-call | bytes 1048576 | tf_op jit(solution)/shard_map/add_left/pallas_call | solution.py:405
Async XLA Ops:
  0.0 3.0 %collective-permute-start = (f32[32,32,128]{2,1,0:T(8,128)}, f32[32,32,128]{2,1,0:T(8,128)S(1)}, u32[]{:S(2)}, u32[]{:S(2)}) collective-permute-start(f32[32,32,128]{2,1,0:T(8,128)} %velocity.1), channel_id=1, source_target_pairs={{0,1},{1,0},{2,3},{3,2},{4,5},{5,4},{6,7},{7,6},{8,9},{9,8},{10,11... | collective-permute-start | bytes 1572872 | tf_op jit(solution)/shard_map/ppermute | solution.py:426
  1.6 1.0 %copy-start = (f32[32,32,128]{2,1,0:T(8,128)S(1)}, f32[32,32,128]{2,1,0:T(8,128)}, u32[]{:S(2)}) copy-start(f32[32,32,128]{2,1,0:T(8,128)} %velocity.1) | copy-start | bytes 1572868
  4.2 9.8 %collective-permute-start.1 = (f32[112,128]{1,0:T(8,128)S(1)}, f32[112,128]{1,0:T(8,128)S(1)}, u32[]{:S(2)}, u32[]{:S(2)}) collective-permute-start(f32[112,128]{1,0:T(8,128)S(1)} %get-tuple-element.26), channel_id=1, source_target_pairs={{0,2},{2,4},{4,6},{6,8},{8,10},{10,12},{12,14},{14,16},{16,18},{18... | collective-permute-start | bytes 172040 | tf_op jit(solution)/shard_map/ppermute | solution.py:458
  6.7 7.3 %collective-permute-start.2 = (f32[16,128]{1,0:T(8,128)S(1)}, f32[16,128]{1,0:T(8,128)S(1)}, u32[]{:S(2)}, u32[]{:S(2)}) collective-permute-start(f32[16,128]{1,0:T(8,128)S(1)} %get-tuple-element.27), channel_id=1, source_target_pairs={{0,4},{2,6},{4,8},{6,10},{8,12},{10,14},{12,16},{14,18},{16,20},{1... | collective-permute-start | bytes 24584 | tf_op jit(solution)/shard_map/ppermute | solution.py:458
  8.2 5.9 %collective-permute-start.3 = (f32[8,128]{1,0:T(8,128)S(1)}, f32[8,128]{1,0:T(8,128)S(1)}, u32[]{:S(2)}, u32[]{:S(2)}) collective-permute-start(f32[8,128]{1,0:T(8,128)S(1)} %get-tuple-element.28), channel_id=1, source_target_pairs={{0,28},{2,30},{4,0},{6,2},{8,4},{10,6},{12,8},{14,10},{16,12},{18,... | collective-permute-start | bytes 12296 | tf_op jit(solution)/shard_map/ppermute | solution.py:458
  11.4 4.3 %collective-permute-start.4 = (f32[128,128]{1,0:T(8,128)S(1)}, f32[128,128]{1,0:T(8,128)S(1)}, u32[]{:S(2)}, u32[]{:S(2)}) collective-permute-start(f32[128,128]{1,0:T(8,128)S(1)} %get-tuple-element.29), channel_id=1, source_target_pairs={{0,30},{2,0},{4,2},{6,4},{8,6},{10,8},{12,10},{14,12},{16,14},{18,... | collective-permute-start | bytes 196616 | tf_op jit(solution)/shard_map/ppermute | solution.py:458
